TPU v7x, 32 devices: a whole 2x2x4 slice. The times are simulated.
32 devices in a mesh: grp: 2 (over x), dev: 16 (over z, y, core).
Axes of the slice: x: 2, y: 2, z: 4, core: 2. Of those that a mesh axis runs over, the one named last changes fastest.
Arguments:
- residual: bfloat16 [64, 8192], P(('grp', 'dev')), parts along dimension 0, may hold values from -8 to 8
- query: bfloat16 [64, 8192], P(('grp', 'dev')), parts along dimension 0, may hold values from -32 to 32
- latest_key_value: bfloat16 [64, 1024], P(('grp', 'dev')), parts along dimension 0, may hold values from -4 to 4
- kv_cache: bfloat16 [128, 256, 1024], P(('grp', 'dev')), parts along dimension 0, may hold values from -4 to 4
- lengths: int32 [128], P(('grp', 'dev')), parts along dimension 0, may hold values from 2 to 256, as said below
- owner_map: int32 [64], P('grp'), parts along dimension 0, may hold values from 0 to 63, as said below
- norm_gain: bfloat16 [8192], replicated, may hold values from 0.099609375 to 1.8984375
- gate_codes: float32 [512, 3, 32768], P(None, None, 'dev'), may hold values from 0 to 16777215, as said below
- gate_scale: bfloat16 [64, 32768], P(None, 'dev'), may hold values from 0.0010986328 to 0.0043945312
- gate_zero: bfloat16 [64, 32768], P(None, 'dev'), may hold values from 6 to 9
- up_codes: float32 [512, 3, 32768], P(None, None, 'dev'), may hold values from 0 to 16777215, as said below
- up_scale: bfloat16 [64, 32768], P(None, 'dev'), may hold values from 0.0010986328 to 0.0043945312
- up_zero: bfloat16 [64, 32768], P(None, 'dev'), may hold values from 6 to 9
- down_codes: float32 [2048, 3, 8192], P('dev'), may hold values from 0 to 16777215, as said below
- down_scale: bfloat16 [256, 8192], P('dev'), may hold values from 0.0005493164 to 0.0021972656
- down_zero: bfloat16 [256, 8192], P('dev'), may hold values from 6 to 9
Outputs:
- layer_output: bfloat16 [64, 8192], P(('grp', 'dev')), parts along dimension 0
There are 2 independent parts, one for each index of `grp`. A program takes and returns all parts, laid end to end along the dimension named above; an argument that names none is the same for every part. Nothing has to cross between parts.
Inputs may be any that keep to these rules, and one draw needn't show every extreme that they name: Batch row r is served by request slot owner_map[r], numbered device * 4 + slot along dev. The values are distinct, so a device serves at most 4 rows, and in every draw some device serves exactly 4; slots that no row names are empty. `lengths`: only slots named by owner_map are read; in every draw some served slot holds exactly 256 tokens. `gate_codes`: every word is a whole number; its base-16 digits are the codes, six in words p = 0 and 1, four in word p = 2. `up_codes`: packed as gate_codes. `down_codes`: packed as gate_codes, rows being hidden units.
All inputs are finite; a program needn't handle non-finite values.
Results may differ from a plain program's by a relative error of at most 0.015.
Values may be sent and summed in bfloat16 or wider, within the bound.
A program may use at most 640 MiB of HBM per device.

v0:
```python
import jax
import jax.numpy as jnp
from jax import lax
from jax.sharding import PartitionSpec as P

QUERY_HEADS = 64
KEY_VALUE_HEADS = 4
HEAD_SIZE = 128


def unpack(packed, zero_point, step_size):
    pieces = []
    for word_slot in range(3):
        digits = 6 if word_slot < 2 else 4
        word = packed[:, word_slot, :]
        for place in range(digits):
            lower = jnp.floor(word / 16.0**place)
            upper = jnp.floor(word / 16.0 ** (place + 1))
            pieces.append(lower - 16.0 * upper)
    nibbles = jnp.stack(pieces, axis=1)
    row_count = packed.shape[0] * 16
    groups = zero_point.shape[0]
    nibbles = nibbles.reshape(groups, row_count // groups, packed.shape[2])
    dequant = (nibbles - zero_point.astype(jnp.float32)[:, None, :]) * step_size.astype(
        jnp.float32
    )[:, None, :]
    return dequant.reshape(row_count, packed.shape[2]).astype(jnp.bfloat16)


def attend_slots(query_rows, incoming_rows, cache_block, lengths):
    count_of_slots = query_rows.shape[0]
    context_span = cache_block.shape[1]
    key_value_width = KEY_VALUE_HEADS * HEAD_SIZE
    group_width = QUERY_HEADS // KEY_VALUE_HEADS
    inv_root = HEAD_SIZE ** (-0.5)
    grouped_heads = query_rows.reshape(count_of_slots, KEY_VALUE_HEADS, group_width, HEAD_SIZE)
    cached_key_rows = cache_block[:, :, :key_value_width].reshape(
        count_of_slots, context_span, KEY_VALUE_HEADS, HEAD_SIZE
    )
    cached_value_rows = cache_block[:, :, key_value_width:].reshape(
        count_of_slots, context_span, KEY_VALUE_HEADS, HEAD_SIZE
    )
    latest_keys = incoming_rows[:, :key_value_width].reshape(
        count_of_slots, KEY_VALUE_HEADS, HEAD_SIZE
    )
    latest_values = incoming_rows[:, key_value_width:].reshape(
        count_of_slots, KEY_VALUE_HEADS, HEAD_SIZE
    )
    scores = (
        jnp.einsum(
            "sghd,stgd->sght", grouped_heads, cached_key_rows, preferred_element_type=jnp.float32
        )
        * inv_root
    )
    own_score = (
        jnp.einsum("sghd,sgd->sgh", grouped_heads, latest_keys, preferred_element_type=jnp.float32)
        * inv_root
    )
    in_cache = (jnp.arange(context_span, dtype=jnp.int32)[None, :] < lengths[:, None])[
        :, None, None, :
    ]
    largest = jnp.maximum(jnp.max(jnp.where(in_cache, scores, -1e30), axis=-1), own_score)
    raised = jnp.where(in_cache, jnp.exp(scores - largest[..., None]), 0.0)
    own_raised = jnp.exp(own_score - largest)
    denominator = jnp.sum(raised, axis=-1) + own_raised
    weights = (raised / denominator[..., None]).astype(jnp.bfloat16)
    own_weight = (own_raised / denominator).astype(jnp.bfloat16)
    attended = jnp.einsum(
        "sght,stgd->sghd", weights, cached_value_rows, preferred_element_type=jnp.float32
    )
    attended = (
        attended
        + own_weight.astype(jnp.float32)[..., None]
        * latest_values.astype(jnp.float32)[:, :, None, :]
    )
    return attended.reshape(count_of_slots, QUERY_HEADS * HEAD_SIZE).astype(jnp.bfloat16)


def local(
    residual,
    query,
    latest_key_value,
    kv_cache,
    lengths,
    owner_map,
    norm_gain,
    gate_codes,
    gate_scale,
    gate_zero,
    up_codes,
    up_scale,
    up_zero,
    down_codes,
    down_scale,
    down_zero,
):
    own_index = lax.axis_index("dev")
    count_of_slots = kv_cache.shape[0]
    row_dev = residual.shape[0]
    ff_local = gate_codes.shape[2]
    slot_ids = own_index * count_of_slots + jnp.arange(count_of_slots, dtype=jnp.int32)
    chooser = (owner_map[None, :] == slot_ids[:, None]).astype(jnp.bfloat16)

    def select_slots(gathered):
        return jnp.dot(chooser, gathered, preferred_element_type=jnp.float32).astype(jnp.bfloat16)

    every_query, every_new, every_stream = (
        lax.all_gather(query, "dev", axis=0, tiled=True),
        lax.all_gather(latest_key_value, "dev", axis=0, tiled=True),
        lax.all_gather(residual, "dev", axis=0, tiled=True),
    )
    stream_slots = select_slots(every_stream)
    attended = attend_slots(select_slots(every_query), select_slots(every_new), kv_cache, lengths)
    w_both = jnp.concatenate(
        [unpack(gate_codes, gate_zero, gate_scale), unpack(up_codes, up_zero, up_scale)], axis=1
    )
    gain_f = norm_gain.astype(jnp.float32)
    slot_stream = (stream_slots.astype(jnp.float32) + attended.astype(jnp.float32)).astype(
        jnp.bfloat16
    )
    every_slot = lax.all_gather(slot_stream, "dev", axis=0, tiled=True)
    stream_all = jnp.take(every_slot, owner_map, axis=0)
    stream_f = stream_all.astype(jnp.float32)
    mean_square = jnp.mean(stream_f * stream_f, axis=-1, keepdims=True)
    normed = (stream_f * lax.rsqrt(mean_square + 1e-05) * gain_f).astype(jnp.bfloat16)
    both = jnp.dot(normed, w_both, preferred_element_type=jnp.float32)
    activated = (jax.nn.silu(both[:, :ff_local]) * both[:, ff_local:]).astype(jnp.bfloat16)
    own_rows = lax.dynamic_slice_in_dim(stream_all, own_index * row_dev, row_dev, 0)
    w_down = unpack(down_codes, down_zero, down_scale)
    products = jnp.dot(activated, w_down, preferred_element_type=jnp.float32)
    placed = lax.dynamic_slice_in_dim(products, own_index * row_dev, row_dev, 0) + own_rows.astype(
        jnp.float32
    )
    products = lax.dynamic_update_slice_in_dim(products, placed, own_index * row_dev, 0)
    feature_block = lax.psum_scatter(products, "dev", scatter_dimension=1, tiled=True).astype(
        jnp.bfloat16
    )
    return lax.all_to_all(feature_block, "dev", split_axis=0, concat_axis=1, tiled=True)


def solution(mesh):
    placed = (
        P(("grp", "dev"), None),
        P(("grp", "dev"), None),
        P(("grp", "dev"), None),
        P(("grp", "dev"), None, None),
        P(("grp", "dev")),
        P("grp"),
        P(),
        P(None, None, "dev"),
        P(None, "dev"),
        P(None, "dev"),
        P(None, None, "dev"),
        P(None, "dev"),
        P(None, "dev"),
        P("dev", None, None),
        P("dev", None),
        P("dev", None),
    )
    return jax.shard_map(
        local, mesh=mesh, in_specs=placed, out_specs=P(("grp", "dev"), None), check_vma=False
    )
```

profile of v0, /device:TPU:0, one launch (start us, length us, event | category | flops | bytes accessed | tf_op | source)
XLA Modules:
  0.0 615.9 jit_solution(7331948858714379310)
XLA Ops:
  6.5 24.9 %all-gather.1 = bf16[16,2,8192]{2,1,0:T(2,128)(2,1)S(1)} all-gather(bf16[1,2,8192]{2,1,0:T(2,128)(2,1)} %bitcast.71), channel_id=1, replica_groups=mesh['grp'=2,'dev'=16] {'dev'}, dimensions={0}, use_global_device_ids=true | all-gather | bytes 557056 | tf_op jit(solution)/shard_map/all_gather | solution.py:108
  35.6 17.6 %all-gather.2 = bf16[16,2,1024]{2,1,0:T(2,128)(2,1)S(1)} all-gather(bf16[1,2,1024]{2,1,0:T(2,128)(2,1)S(1)} %bitcast.75), channel_id=1, replica_groups=mesh['grp'=2,'dev'=16] {'dev'}, dimensions={0}, use_global_device_ids=true | all-gather | bytes 69632 | tf_op jit(solution)/shard_map/all_gather | solution.py:109
  54.8 20.3 %all-gather = bf16[16,2,8192]{2,1,0:T(2,128)(2,1)S(1)} all-gather(bf16[1,2,8192]{2,1,0:T(2,128)(2,1)S(1)} %bitcast.72), channel_id=1, replica_groups=mesh['grp'=2,'dev'=16] {'dev'}, dimensions={0}, use_global_device_ids=true | all-gather | bytes 557056 | tf_op jit(solution)/shard_map/all_gather | solution.py:110
  76.9 5.2 subtract_dynamic-update-slice_fusion.47
  82.1 5.3 subtract_dynamic-update-slice_fusion.46
  87.4 5.3 subtract_dynamic-update-slice_fusion.45
  123.3 3.1 subtract_dynamic-update-slice_fusion.33
  129.2 56.5 %copy.50 = f32[512,16,2048]{2,1,0:T(8,128)} copy(f32[512,16,2048]{2,0,1:T(8,128)} %subtract_dynamic-update-slice_fusion.32) | data formatting | bytes 134217728 | tf_op jit(solution)/shard_map/stack | solution.py:20
  185.7 5.2 subtract_dynamic-update-slice_fusion.31
  190.9 5.3 subtract_dynamic-update-slice_fusion.30
  196.2 5.3 subtract_dynamic-update-slice_fusion.29
  232.1 2.9 subtract_dynamic-update-slice_fusion.17
  237.8 56.6 %copy.51 = f32[512,16,2048]{2,1,0:T(8,128)} copy(f32[512,16,2048]{2,0,1:T(8,128)} %subtract_dynamic-update-slice_fusion.16) | data formatting | bytes 134217728 | tf_op jit(solution)/shard_map/stack | solution.py:20
  295.2 5.0 subtract_dynamic-update-slice_fusion.15
  300.2 5.1 subtract_dynamic-update-slice_fusion.14
  305.3 5.2 subtract_dynamic-update-slice_fusion.13
  341.0 3.0 subtract_dynamic-update-slice_fusion.1
  346.8 56.4 %copy.52 = f32[128,16,8192]{2,1,0:T(8,128)} copy(f32[128,16,8192]{2,0,1:T(8,128)} %subtract_dynamic-update-slice_fusion) | data formatting | bytes 134217728 | tf_op jit(solution)/shard_map/stack | solution.py:20
  403.3 33.4 %fusion.4 = bf16[2048,8192]{1,0:T(8,128)(2,1)} fusion(f32[128,16,8192]{2,1,0:T(8,128)} %copy.52, f32[16,8192]{1,0:T(8,128)S(1)} %convert_element_type.114, f32[16,8192]{1,0:T(8,128)S(1)} %convert_element_type.113), kind=kLoop, calls=%fused_computation.6 | loop fusion | flops 50331648 | bytes 101711872 | tf_op jit(solution)/shard_map/convert_element_type | solution.py:27
  436.7 65.2 %fusion.5 = (bf16[8192,2048]{1,0:T(8,128)(2,1)}, bf16[8192,2048]{1,0:T(8,128)(2,1)}) fusion(f32[512,16,2048]{2,1,0:T(8,128)} %copy.51, f32[64,2048]{1,0:T(8,128)S(1)} %convert_element_type.110, f32[64,2048]{1,0:T(8,128)S(1)} %convert_element_type.109, f32[64,2048]{1,0:T(8,128)S(1)} %convert_element_type.107, f32[64,2048]{1,0:T(8,128)S(1)} %convert_element_type.106, ...), kind=kLoop, calls=%fused_computation.9 | loop fusion | flops 100663296 | bytes 203423744 | tf_op jit(solution)/shard_map/convert_element_type | solution.py:27
  504.5 23.2 %fusion = f32[32,4096]{1,0:T(8,128)S(1)} fusion(bf16[8192,2048]{1,0:T(8,128)(2,1)} %get-tuple-element.15, bf16[8192,2048]{1,0:T(8,128)(2,1)} %get-tuple-element.16, bf16[32,8192]{1,0:T(8,128)(2,1)S(1)} %get-tuple-element.6, f32[8192]{0:T(1024)S(1)} %copy-done.8, f32[32]{0:T(128)S(1)} %add_rsqrt_fusion), kind=kOutput, calls=%fused_computation.1 | convolution fusion | flops 2282749952 | bytes 68190336 | tf_op jit(solution)/shard_map/dot_general | solution.py:126
  527.7 13.5 %fusion.22 = f32[32,8192]{1,0:T(8,128)S(1)} fusion(bf16[2048,8192]{1,0:T(8,128)(2,1)} %fusion.4, f32[32,4096]{1,0:T(8,128)S(1)} %fusion), kind=kOutput, calls=%fused_computation.127 | convolution fusion | flops 1074135040 | bytes 35127296 | tf_op jit(solution)/shard_map/dot_general | solution.py:130
  542.4 54.8 %reduce-scatter.2.cloned.1.call-done = f32[32,512]{1,0:T(8,128)} async-done(((f32[32,8192]{1,0:T(8,128)}), f32[32,512]{1,0:T(8,128)}) %reduce-scatter.2.cloned.1.call-update) | async-done | bytes 65552 | tf_op jit(solution)/shard_map/reduce_scatter | solution.py:135
  598.1 10.1 %all_to_all.19 = bf16[16,2,512]{2,1,0:T(2,128)(2,1)S(1)} all-to-all(bf16[16,2,512]{2,1,0:T(2,128)(2,1)S(1)} %all_to_all.14), channel_id=1, replica_groups=mesh['grp'=2,'dev'=16] {'dev'}, dimensions={0} | all-to-all | bytes 65536 | tf_op jit(solution)/shard_map/all_to_all | solution.py:138
  (127 shorter events, 113.4 us)
Async XLA Ops:
  6.5 495.4 %all-gather.6.cloned.1.call-start = ((), (), s32[]{:S(2)}) async-start(), calls=%async_computation.3 | async-start | bytes 1114112 | tf_op jit(solution)/shard_map/all_gather | solution.py:121
  6.5 29.1 %copy-start.10 = (bf16[2,1024]{1,0:T(2,128)(2,1)S(1)}, bf16[2,1024]{1,0:T(2,128)(2,1)}, u32[]{:S(2)}) copy-start(bf16[2,1024]{1,0:T(2,128)(2,1)} %param.18) | copy-start | bytes 12292
  31.4 21.8 %copy-start.11 = (s32[32]{0:T(128)S(1)}, s32[32]{0:T(128)}, u32[]{:S(2)}) copy-start(s32[32]{0:T(128)} %param.21) | copy-start | bytes 388
  35.1 19.7 %copy-start.7 = (bf16[2,8192]{1,0:T(2,128)(2,1)S(1)}, bf16[2,8192]{1,0:T(2,128)(2,1)}, u32[]{:S(2)}) copy-start(bf16[2,8192]{1,0:T(2,128)(2,1)} %param.16) | copy-start | bytes 98308
  76.7 520.5 %reduce-scatter.2.cloned.1.call-start = ((), (), s32[]{:S(2)}) async-start(), calls=%async_computation.2 | async-start | bytes 1114112 | tf_op jit(solution)/shard_map/reduce_scatter | solution.py:135
  76.9 15.8 %slice-start = ((s8[12582912]{0:T(1024)(128)(4,1)}), s8[4194304]{0:T(1024)(128)(4,1)S(1)}, s32[]{:S(2)}) async-start(s8[12582912]{0:T(1024)(128)(4,1)} %bitcast.59), calls=%async_computation.4 | async-start | bytes 8388608
  82.1 10.6 %slice-start.1 = ((s8[12582912]{0:T(1024)(128)(4,1)}), s8[4194304]{0:T(1024)(128)(4,1)S(1)}, s32[]{:S(2)}) async-start(s8[12582912]{0:T(1024)(128)(4,1)} %bitcast.59), calls=%async_computation.5 | async-start | bytes 8388608
  87.4 5.3 slice-start.2
  185.7 15.8 %slice-start.3 = ((s8[12582912]{0:T(1024)(128)(4,1)}), s8[4194304]{0:T(1024)(128)(4,1)S(1)}, s32[]{:S(2)}) async-start(s8[12582912]{0:T(1024)(128)(4,1)} %bitcast.61), calls=%async_computation.7 | async-start | bytes 8388608
  190.9 10.6 %slice-start.4 = ((s8[12582912]{0:T(1024)(128)(4,1)}), s8[4194304]{0:T(1024)(128)(4,1)S(1)}, s32[]{:S(2)}) async-start(s8[12582912]{0:T(1024)(128)(4,1)} %bitcast.61), calls=%async_computation.8 | async-start | bytes 8388608
  196.2 5.3 slice-start.5
  237.8 56.6 %copy-start.1 = (bf16[64,2048]{1,0:T(8,128)(2,1)S(1)}, bf16[64,2048]{1,0:T(8,128)(2,1)}, u32[]{:S(2)}) copy-start(bf16[64,2048]{1,0:T(8,128)(2,1)} %param.25) | copy-start | bytes 786436
  237.8 56.6 %copy-start.2 = (bf16[64,2048]{1,0:T(8,128)(2,1)S(1)}, bf16[64,2048]{1,0:T(8,128)(2,1)}, u32[]{:S(2)}) copy-start(bf16[64,2048]{1,0:T(8,128)(2,1)} %param.24) | copy-start | bytes 786436
  237.8 56.7 %copy-start.3 = (bf16[64,2048]{1,0:T(8,128)(2,1)S(1)}, bf16[64,2048]{1,0:T(8,128)(2,1)}, u32[]{:S(2)}) copy-start(bf16[64,2048]{1,0:T(8,128)(2,1)} %param.28) | copy-start | bytes 786436
  237.8 56.7 %copy-start.4 = (bf16[64,2048]{1,0:T(8,128)(2,1)S(1)}, bf16[64,2048]{1,0:T(8,128)(2,1)}, u32[]{:S(2)}) copy-start(bf16[64,2048]{1,0:T(8,128)(2,1)} %param.27) | copy-start | bytes 786436
  237.8 56.8 %copy-start.9 = (bf16[8192]{0:T(1024)(128)(2,1)S(1)}, bf16[8192]{0:T(1024)(128)(2,1)}, u32[]{:S(2)}) copy-start(bf16[8192]{0:T(1024)(128)(2,1)} %param.22) | copy-start | bytes 49156
  295.2 15.3 %slice-start.6 = ((s8[12582912]{0:T(1024)(128)(4,1)}), s8[4194304]{0:T(1024)(128)(4,1)S(1)}, s32[]{:S(2)}) async-start(s8[12582912]{0:T(1024)(128)(4,1)} %bitcast.63), calls=%async_computation.10 | async-start | bytes 8388608
  300.2 10.3 %slice-start.7 = ((s8[12582912]{0:T(1024)(128)(4,1)}), s8[4194304]{0:T(1024)(128)(4,1)S(1)}, s32[]{:S(2)}) async-start(s8[12582912]{0:T(1024)(128)(4,1)} %bitcast.63), calls=%async_computation.11 | async-start | bytes 8388608
  305.3 5.2 slice-start.8
  346.8 56.4 %copy-start.5 = (bf16[16,8192]{1,0:T(8,128)(2,1)S(1)}, bf16[16,8192]{1,0:T(8,128)(2,1)}, u32[]{:S(2)}) copy-start(bf16[16,8192]{1,0:T(8,128)(2,1)} %param.31) | copy-start | bytes 786436
  346.8 56.5 %copy-start.6 = (bf16[16,8192]{1,0:T(8,128)(2,1)S(1)}, bf16[16,8192]{1,0:T(8,128)(2,1)}, u32[]{:S(2)}) copy-start(bf16[16,8192]{1,0:T(8,128)(2,1)} %param.30) | copy-start | bytes 786436
  436.7 65.2 %copy-start.12 = (s32[32]{0:T(128)S(1)}, s32[32]{0:T(128)}, u32[]{:S(2)}) copy-start(s32[32]{0:T(128)} %param.21) | copy-start | bytes 388
  501.9 2.7 copy-start.8
  541.3 1.0 copy-start
Sparse Core Ops, SparseCore 0:
  76.8 35.2 all-gather.5
  542.5 54.6 reduce-scatter.1
where the time goes:
time: 619 us; the launch traced here: 616 us
  other arithmetic  258 us (42%)
  local copies, waits for them, and re-layouts  177 us (29%)
  blocking collectives  73 us (12%)
  waiting for transfers between devices  54.9 us (9%)
  matrix products  39.6 us (6%)
  between operations  14 us (2%)
    another operation x3, local copies, waits for them, and re-layouts, unpack(): nibbles = jnp.stack(pieces, axis=1)  169 us
    unnamed x48, other arithmetic  148 us
    convert_element_type x2, other arithmetic, unpack(): return dequant.reshape(row_count, packed.shape[2]).astype(jnp.bfloat16)  98.6 us
    reduce_scatter x1, waiting for transfers between devices, local(): lax.psum_scatter(products, 'dev', scatter_dimension=1, tiled=True)  54.8 us
    all_gather x1, blocking collectives, local(): lax.all_gather(query, 'dev', axis=0, tiled=True)  24.9 us
    dot_general x1, matrix products, local(): both = jnp.dot(normed, w_both, preferred_element_type=jnp.float32)  23.2 us
    all_gather x1, blocking collectives, local(): lax.all_gather(residual, 'dev', axis=0, tiled=True)  20.3 us
    all_gather x1, blocking collectives, local(): lax.all_gather(latest_key_value, 'dev', axis=0, tiled=True)  17.6 us
  transfers between devices with their start and end apart: 2, of which 1 were waited for; matrix products, arithmetic and copies ran while one was open for 69% of the time, Pallas kernels for 0%

commit v1 on v0

--- a/solution.py
+++ b/solution.py
@@ -1,30 +1,146 @@
+import functools
 import jax
 import jax.numpy as jnp
 from jax import lax
+from jax.experimental import pallas as pl
+from jax.experimental.pallas import tpu as pltpu
 from jax.sharding import PartitionSpec as P
 
 QUERY_HEADS = 64
 KEY_VALUE_HEADS = 4
 HEAD_SIZE = 128
-
-
-def unpack(packed, zero_point, step_size):
+PLACES = tuple((p, k) for p in range(3) for k in range(6 if p < 2 else 4))
+
+
+def order_matrix():
+    row = lax.broadcasted_iota(jnp.int32, (256, 256), 0)
+    col = lax.broadcasted_iota(jnp.int32, (256, 256), 1)
+    m = col // 16
+    hit = row == (col % 16) * 16 + m
+    place = jnp.where(m < 6, m, jnp.where(m < 12, m - 6, m - 12))
+    value = jnp.zeros((256, 256), jnp.float32)
+    for k in range(6):
+        value = jnp.where(place == k, 16.0**-k, value)
+    return jnp.where(hit, value, 0.0).astype(jnp.bfloat16)
+
+
+def unpack_chunk(words_ref, t, scale, zero):
     pieces = []
-    for word_slot in range(3):
-        digits = 6 if word_slot < 2 else 4
-        word = packed[:, word_slot, :]
-        for place in range(digits):
-            lower = jnp.floor(word / 16.0**place)
-            upper = jnp.floor(word / 16.0 ** (place + 1))
-            pieces.append(lower - 16.0 * upper)
-    nibbles = jnp.stack(pieces, axis=1)
-    row_count = packed.shape[0] * 16
-    groups = zero_point.shape[0]
-    nibbles = nibbles.reshape(groups, row_count // groups, packed.shape[2])
-    dequant = (nibbles - zero_point.astype(jnp.float32)[:, None, :]) * step_size.astype(
-        jnp.float32
-    )[:, None, :]
-    return dequant.reshape(row_count, packed.shape[2]).astype(jnp.bfloat16)
+    zeros = [zero * 16.0**k for k in range(6)]
+    for p in range(3):
+        word = words_ref[p, pl.ds(t * 16, 16), :].astype(jnp.int32)
+        for k in range(6 if p < 2 else 4):
+            digit = (word & (15 << (4 * k))).astype(jnp.float32).astype(jnp.bfloat16)
+            pieces.append((digit - zeros[k]) * scale)
+    return jnp.concatenate(pieces, axis=0)
+
+
+def rows_of(ref, t, n):
+    two = ref[t]
+    first = jnp.broadcast_to(two[0:1, :], (8, n))
+    second = jnp.broadcast_to(two[1:2, :], (8, n))
+    return jnp.concatenate([first, second], axis=0).astype(jnp.bfloat16)
+
+
+def reorder(x_ref, xp_ref, chunks):
+    order = order_matrix()
+
+    def one(t, carry):
+        block = x_ref[:, pl.ds(pl.multiple_of(t * 256, 256), 256)]
+        xp_ref[t] = jnp.dot(block, order, preferred_element_type=jnp.float32).astype(jnp.bfloat16)
+        return carry
+
+    lax.fori_loop(0, chunks, one, 0)
+
+
+def gate_up_kernel(chunks, x_ref, gc, gs, gz, uc, us, uz, out_ref, xp_ref):
+    rows, n = out_ref.shape
+
+    @pl.when(pl.program_id(0) == 0)
+    def _():
+        reorder(x_ref, xp_ref, chunks)
+
+    def step(t, sums):
+        x = xp_ref[t]
+        new = []
+        for total, c, s, z in zip(sums, (gc, uc), (gs, us), (gz, uz)):
+            w = unpack_chunk(c, t, rows_of(s, t, n), rows_of(z, t, n))
+            new.append(total + jnp.dot(x, w, preferred_element_type=jnp.float32))
+        return tuple(new)
+
+    start = jnp.zeros((rows, n), jnp.float32)
+    gate, up = lax.fori_loop(0, chunks, step, (start, start))
+    out_ref[...] = (gate / (1.0 + jnp.exp(-gate)) * up).astype(jnp.bfloat16)
+
+
+def down_kernel(chunks, x_ref, c, s, z, out_ref, xp_ref):
+    rows, n = out_ref.shape
+
+    @pl.when(pl.program_id(0) == 0)
+    def _():
+        reorder(x_ref, xp_ref, chunks)
+
+    def step(t, total):
+        w = unpack_chunk(c, t, rows_of(s, t, n), rows_of(z, t, n))
+        return total + jnp.dot(xp_ref[t], w, preferred_element_type=jnp.float32)
+
+    out_ref[...] = lax.fori_loop(0, chunks, step, jnp.zeros((rows, n), jnp.float32))
+
+
+def words_spec(words, n):
+    return pl.BlockSpec((3, words, n), lambda j: (0, 0, j))
+
+
+def pairs_spec(pairs, n):
+    return pl.BlockSpec((pairs, 2, n), lambda j: (0, 0, j))
+
+
+def gate_up(x, gate, up, n):
+    rows, depth = x.shape
+    width = gate[0].shape[2]
+    n = min(n, width)
+    chunks = depth // 256
+    args = [x]
+    specs = [pl.BlockSpec((rows, depth), lambda j: (0, 0))]
+    for codes, scale, zero in (gate, up):
+        args += [codes.transpose(1, 0, 2)]
+        args += [v.astype(jnp.float32).reshape(chunks, 2, width) for v in (scale, zero)]
+        specs += [words_spec(depth // 16, n), pairs_spec(chunks, n), pairs_spec(chunks, n)]
+    return pl.pallas_call(
+        functools.partial(gate_up_kernel, chunks),
+        grid=(width // n,),
+        out_shape=jax.ShapeDtypeStruct((rows, width), jnp.bfloat16),
+        in_specs=specs,
+        out_specs=pl.BlockSpec((rows, n), lambda j: (0, j)),
+        scratch_shapes=[pltpu.VMEM((chunks, rows, 256), jnp.bfloat16)],
+        compiler_params=pltpu.CompilerParams(vmem_limit_bytes=48 << 20),
+        name="gate_up",
+    )(*args)
+
+
+def down(x, codes, scale, zero, n):
+    rows, depth = x.shape
+    width = codes.shape[2]
+    chunks = depth // 256
+    return pl.pallas_call(
+        functools.partial(down_kernel, chunks),
+        grid=(width // n,),
+        out_shape=jax.ShapeDtypeStruct((rows, width), jnp.float32),
+        in_specs=[
+            pl.BlockSpec((rows, depth), lambda j: (0, 0)),
+            words_spec(depth // 16, n),
+            pairs_spec(chunks, n),
+            pairs_spec(chunks, n),
+        ],
+        out_specs=pl.BlockSpec((rows, n), lambda j: (0, j)),
+        scratch_shapes=[pltpu.VMEM((chunks, rows, 256), jnp.bfloat16)],
+        compiler_params=pltpu.CompilerParams(vmem_limit_bytes=48 << 20),
+        name="down",
+    )(
+        x,
+        codes.transpose(1, 0, 2),
+        *[v.astype(jnp.float32).reshape(chunks, 2, width) for v in (scale, zero)],
+    )
 
 
 def attend_slots(query_rows, incoming_rows, cache_block, lengths):
@@ -96,8 +212,6 @@
 ):
     own_index = lax.axis_index("dev")
     count_of_slots = kv_cache.shape[0]
-    row_dev = residual.shape[0]
-    ff_local = gate_codes.shape[2]
     slot_ids = own_index * count_of_slots + jnp.arange(count_of_slots, dtype=jnp.int32)
     chooser = (owner_map[None, :] == slot_ids[:, None]).astype(jnp.bfloat16)
 
@@ -111,9 +225,6 @@
     )
     stream_slots = select_slots(every_stream)
     attended = attend_slots(select_slots(every_query), select_slots(every_new), kv_cache, lengths)
-    w_both = jnp.concatenate(
-        [unpack(gate_codes, gate_zero, gate_scale), unpack(up_codes, up_zero, up_scale)], axis=1
-    )
     gain_f = norm_gain.astype(jnp.float32)
     slot_stream = (stream_slots.astype(jnp.float32) + attended.astype(jnp.float32)).astype(
         jnp.bfloat16
@@ -123,19 +234,14 @@
     stream_f = stream_all.astype(jnp.float32)
     mean_square = jnp.mean(stream_f * stream_f, axis=-1, keepdims=True)
     normed = (stream_f * lax.rsqrt(mean_square + 1e-05) * gain_f).astype(jnp.bfloat16)
-    both = jnp.dot(normed, w_both, preferred_element_type=jnp.float32)
-    activated = (jax.nn.silu(both[:, :ff_local]) * both[:, ff_local:]).astype(jnp.bfloat16)
+    activated = gate_up(
+        normed, (gate_codes, gate_scale, gate_zero), (up_codes, up_scale, up_zero), 256
+    )
+    products = down(activated, down_codes, down_scale, down_zero, 512)
+    row_dev = residual.shape[0]
     own_rows = lax.dynamic_slice_in_dim(stream_all, own_index * row_dev, row_dev, 0)
-    w_down = unpack(down_codes, down_zero, down_scale)
-    products = jnp.dot(activated, w_down, preferred_element_type=jnp.float32)
-    placed = lax.dynamic_slice_in_dim(products, own_index * row_dev, row_dev, 0) + own_rows.astype(
-        jnp.float32
-    )
-    products = lax.dynamic_update_slice_in_dim(products, placed, own_index * row_dev, 0)
-    feature_block = lax.psum_scatter(products, "dev", scatter_dimension=1, tiled=True).astype(
-        jnp.bfloat16
-    )
-    return lax.all_to_all(feature_block, "dev", split_axis=0, concat_axis=1, tiled=True)
+    summed = lax.psum_scatter(products, "dev", scatter_dimension=0, tiled=True)
+    return (own_rows.astype(jnp.float32) + summed).astype(jnp.bfloat16)
 
 
 def solution(mesh):

time: 619 us -> 310 us (0.50)
  other arithmetic: 258 us -> 4.24 us
  local copies, waits for them, and re-layouts: 177 us -> 16.9 us
  Pallas kernels: 0 us -> 87.6 us
  waiting for transfers between devices: 54.9 us -> 120 us
  matrix products: 39.6 us -> 3.56 us
  blocking collectives: 73 us -> 63.1 us
    another operation x3 -> x0, local copies, waits for them, and re-layouts: 169 us -> none  [unpack(): nibbles = jnp.stack(pieces, axis=1)]
    unnamed x48 -> x0, other arithmetic: 148 us -> none
    convert_element_type x9 -> x2, other arithmetic: 99.6 us -> 1.85 us  [the longest x1 1.66 us: local(): return (own_rows.astype(jnp.float32) + summed).astype(jnp.bfloat16)]
    unnamed x2 -> x3, waiting for transfers between devices: 0.03 us -> 91.2 us
    pallas_call x0 -> x2, Pallas kernels: none -> 87.6 us  [the longest x1 58.7 us: gate_up(): pl.pallas_call(functools.partial(gate_up_kernel, chunks), grid=(width //...]
    reduce_scatter x1 -> x0, waiting for transfers between devices: 54.8 us -> none  [local(): lax.psum_scatter(products, 'dev', scatter_dimension=1, tiled=True)]
    dot_general x2 -> x0, matrix products: 36.7 us -> none  [the longest x1 23.2 us: local(): both = jnp.dot(normed, w_both, preferred_element_type=jnp.float32)]
    all_gather x1, waiting for transfers between devices: 0.02 us -> 28.5 us  [local(): every_slot = lax.all_gather(slot_stream, 'dev', axis=0, tiled=True)]
  transfers between devices with their start and end apart: 2 -> 2, of which waited for: 1 -> 2; matrix products, arithmetic and copies ran while one was open for 69% -> 2% of each run, Pallas kernels for 0% -> 0%
where the time goes in v1:
time: 310 us; the launch traced here: 309 us
  waiting for transfers between devices  120 us (39%)
  Pallas kernels  87.6 us (28%)
  blocking collectives  63.1 us (20%)
  local copies, waits for them, and re-layouts  16.9 us (5%)
  between operations  14.3 us (5%)
  other arithmetic  4.24 us (1%)
  matrix products  3.56 us (1%)
    unnamed x3, waiting for transfers between devices  91.2 us
    pallas_call x1, Pallas kernels, gate_up(): pl.pallas_call(functools.partial(gate_up_kernel, chunks), grid=(width //...  58.7 us
    pallas_call x1, Pallas kernels, down(): pl.pallas_call(functools.partial(down_kernel, chunks), grid=(width // n,)...  28.8 us
    all_gather x1, waiting for transfers between devices, local(): every_slot = lax.all_gather(slot_stream, 'dev', axis=0, tiled=True)  28.5 us
    all_gather x1, blocking collectives, local(): lax.all_gather(query, 'dev', axis=0, tiled=True)  24.9 us
    all_gather x1, blocking collectives, local(): lax.all_gather(residual, 'dev', axis=0, tiled=True)  20.2 us
    all_gather x1, blocking collectives, local(): lax.all_gather(latest_key_value, 'dev', axis=0, tiled=True)  17.9 us
  transfers between devices with their start and end apart: 2, of which 2 were waited for; matrix products, arithmetic and copies ran while one was open for 2% of the time, Pallas kernels for 0%

profile of v1, /device:TPU:0, one launch (start us, length us, event | category | flops | bytes accessed | tf_op | source)
XLA Modules:
  0.0 309.3 jit_solution(9856007412643675964)
XLA Ops:
  6.6 24.9 %all-gather.1 = bf16[16,2,8192]{2,1,0:T(2,128)(2,1)S(1)} all-gather(bf16[1,2,8192]{2,1,0:T(2,128)(2,1)} %bitcast.37), channel_id=1, replica_groups=mesh['grp'=2,'dev'=16] {'dev'}, dimensions={0}, use_global_device_ids=true | all-gather | bytes 557056 | tf_op jit(solution)/shard_map/all_gather | solution.py:222
  31.7 0.9 fusion.6
  32.7 0.7 iota_compare_fusion
  33.4 1.8 fusion.28
  35.2 0.5 copy.29
  35.7 17.9 %all-gather.2 = bf16[16,2,1024]{2,1,0:T(2,128)(2,1)S(1)} all-gather(bf16[1,2,1024]{2,1,0:T(2,128)(2,1)} %bitcast.41), channel_id=1, replica_groups=mesh['grp'=2,'dev'=16] {'dev'}, dimensions={0}, use_global_device_ids=true | all-gather | bytes 69632 | tf_op jit(solution)/shard_map/all_gather | solution.py:223
  53.6 0.8 convolution_convert_fusion.2
  55.8 20.2 %all-gather = bf16[16,2,8192]{2,1,0:T(2,128)(2,1)S(1)} all-gather(bf16[1,2,8192]{2,1,0:T(2,128)(2,1)S(1)} %bitcast.38), channel_id=1, replica_groups=mesh['grp'=2,'dev'=16] {'dev'}, dimensions={0}, use_global_device_ids=true | all-gather | bytes 557056 | tf_op jit(solution)/shard_map/all_gather | solution.py:224
  76.7 0.9 fusion.3
  78.0 1.3 reshape.114.gz
  79.3 1.3 reshape.116.us
  80.6 1.3 reshape.118.uz
  81.9 1.3 reshape.120.s
  83.2 1.3 reshape.122.z
  84.5 28.5 %all-gather.6.cloned.1.call-done = bf16[16,4,8192]{2,1,0:T(4,128)(2,1)} async-done(((bf16[1,4,8192]{2,1,0:T(4,128)(2,1)}), bf16[16,4,8192]{2,1,0:T(4,128)(2,1)}) %all-gather.6.cloned.1.call-update) | async-done | bytes 1048592 | tf_op jit(solution)/shard_map/all_gather | solution.py:232
  113.0 2.2 reshape.139
  115.2 3.5 %gather_fusion = bf16[32,8192]{1,0:T(8,128)(2,1)} fusion(bf16[64,8192]{1,0:T(8,128)(2,1)} %reshape.139, s32[1024]{0:T(1024)S(1)} %pad_clamp_fusion), kind=kCustom, calls=%fused_computation | custom fusion | bytes 1048704 | tf_op jit(solution)/shard_map/jit(_take)/gather | solution.py:233
  118.6 1.4 fusion.7
  120.2 0.6 copy-done
  120.8 58.7 %gate_up.1.x_ref = bf16[32,2048]{1,0:T(8,128)(2,1)S(1)} custom-call(bf16[32,8192]{1,0:T(8,128)(2,1)S(1)} %fusion.9.x_ref, f32[3,512,2048]{2,1,0:T(8,128)} %bitcast.29, f32[32,2,2048]{2,1,0:T(2,128)S(1)} %reshape.112.gs, f32[32,2,2048]{2,1,0:T(2,128)S(1)} %reshape.114.gz, f32[3,512,2048]{2,1,0:T(8,128)} %bitcast.30, f32[32,2,2048]{2,1,0:T(2,128)S(1)} %reshape.116.us, ...), custom_call_target="tpu_custom_call" | custom-call | tf_op jit(solution)/shard_map/gate_up/pallas_call | solution.py:109
  179.6 28.8 %down.1 = f32[32,8192]{1,0:T(8,128)} custom-call(bf16[32,2048]{1,0:T(8,128)(2,1)S(1)} %gate_up.1.x_ref, f32[3,128,8192]{2,1,0:T(8,128)} %bitcast.31, f32[8,2,8192]{2,1,0:T(2,128)S(1)} %reshape.120.s, f32[8,2,8192]{2,1,0:T(2,128)S(1)} %reshape.122.z), custom_call_target="tpu_custom_call" | custom-call | tf_op jit(solution)/shard_map/down/pallas_call | solution.py:125
  208.4 0.6 dynamic-slice
  209.7 91.2 %all-reduce.3.cloned.1.call-done = f32[32,8192]{1,0:T(8,128)} async-done(((f32[32,8192]{1,0:T(8,128)}), f32[32,8192]{1,0:T(8,128)}) %all-reduce.3.cloned.1.call-update) | async-done | bytes 1048592
  300.8 1.7 fusion.15
  (37 shorter events, 2.8 us)
Async XLA Ops:
  6.5 70.1 %copy-start.4 = (s32[32]{0:T(128)S(1)}, s32[32]{0:T(128)}, u32[]{:S(2)}) copy-start(s32[32]{0:T(128)} %param.21) | copy-start | bytes 388
  6.5 49.2 %copy-start.2 = (bf16[2,8192]{1,0:T(2,128)(2,1)S(1)}, bf16[2,8192]{1,0:T(2,128)(2,1)}, u32[]{:S(2)}) copy-start(bf16[2,8192]{1,0:T(2,128)(2,1)} %param.16) | copy-start | bytes 98308
  6.5 71.1 %copy-start.3 = (bf16[8192]{0:T(1024)(128)(2,1)S(1)}, bf16[8192]{0:T(1024)(128)(2,1)}, u32[]{:S(2)}) copy-start(bf16[8192]{0:T(1024)(128)(2,1)} %param.22) | copy-start | bytes 49156
  6.5 71.1 %copy-start.1 = (bf16[64,2048]{1,0:T(8,128)(2,1)S(1)}, bf16[64,2048]{1,0:T(8,128)(2,1)}, u32[]{:S(2)}) copy-start(bf16[64,2048]{1,0:T(8,128)(2,1)} %param.24) | copy-start | bytes 786436
  6.5 106.4 %all-gather.6.cloned.1.call-start = ((), (), s32[]{:S(2)}) async-start(), calls=%async_computation | async-start | bytes 1114112 | tf_op jit(solution)/shard_map/all_gather | solution.py:232
  77.6 223.2 %all-reduce.3.cloned.1.call-start = ((), (), s32[]{:S(2)}) async-start(), calls=%async_computation.1 | async-start | bytes 2097152
  120.0 0.8 copy-start
  179.6 28.9 %copy-start.5 = (u32[32]{0:T(128)S(1)}, u32[32]{0:T(128)}, u32[]{:S(2)}) copy-start(u32[32]{0:T(128)} %constant.48) | copy-start | bytes 388
Sparse Core Ops, SparseCore 0:
  77.7 35.2 all-gather.5
  208.5 92.2 all-reduce.2

commit v2 on v1

--- a/solution.py
+++ b/solution.py
@@ -36,9 +36,8 @@
 
 
 def rows_of(ref, t, n):
-    two = ref[t]
-    first = jnp.broadcast_to(two[0:1, :], (8, n))
-    second = jnp.broadcast_to(two[1:2, :], (8, n))
+    first = jnp.broadcast_to(ref[pl.ds(2 * t, 1), :], (8, n))
+    second = jnp.broadcast_to(ref[pl.ds(2 * t + 1, 1), :], (8, n))
     return jnp.concatenate([first, second], axis=0).astype(jnp.bfloat16)
 
 
@@ -53,8 +52,14 @@
     lax.fori_loop(0, chunks, one, 0)
 
 
-def gate_up_kernel(chunks, x_ref, gc, gs, gz, uc, us, uz, out_ref, xp_ref):
+def widen(sources, targets):
+    for source, target in zip(sources, targets):
+        target[...] = source[...].astype(jnp.float32)
+
+
+def gate_up_kernel(chunks, x_ref, gc, gs_in, gz_in, uc, us_in, uz_in, out_ref, xp_ref, gs, gz, us, uz):
     rows, n = out_ref.shape
+    widen((gs_in, gz_in, us_in, uz_in), (gs, gz, us, uz))
 
     @pl.when(pl.program_id(0) == 0)
     def _():
@@ -73,8 +78,9 @@
     out_ref[...] = (gate / (1.0 + jnp.exp(-gate)) * up).astype(jnp.bfloat16)
 
 
-def down_kernel(chunks, x_ref, c, s, z, out_ref, xp_ref):
+def down_kernel(chunks, x_ref, c, s_in, z_in, out_ref, xp_ref, s, z):
     rows, n = out_ref.shape
+    widen((s_in, z_in), (s, z))
 
     @pl.when(pl.program_id(0) == 0)
     def _():
@@ -84,7 +90,8 @@
         w = unpack_chunk(c, t, rows_of(s, t, n), rows_of(z, t, n))
         return total + jnp.dot(xp_ref[t], w, preferred_element_type=jnp.float32)
 
-    out_ref[...] = lax.fori_loop(0, chunks, step, jnp.zeros((rows, n), jnp.float32))
+    total = lax.fori_loop(0, chunks, step, jnp.zeros((rows, n), jnp.float32))
+    out_ref[...] = total.astype(jnp.bfloat16)
 
 
 def words_spec(words, n):
@@ -92,7 +99,7 @@
 
 
 def pairs_spec(pairs, n):
-    return pl.BlockSpec((pairs, 2, n), lambda j: (0, 0, j))
+    return pl.BlockSpec((2 * pairs, n), lambda j: (0, j))
 
 
 def gate_up(x, gate, up, n):
@@ -104,7 +111,7 @@
     specs = [pl.BlockSpec((rows, depth), lambda j: (0, 0))]
     for codes, scale, zero in (gate, up):
         args += [codes.transpose(1, 0, 2)]
-        args += [v.astype(jnp.float32).reshape(chunks, 2, width) for v in (scale, zero)]
+        args += [scale, zero]
         specs += [words_spec(depth // 16, n), pairs_spec(chunks, n), pairs_spec(chunks, n)]
     return pl.pallas_call(
         functools.partial(gate_up_kernel, chunks),
@@ -112,7 +119,8 @@
         out_shape=jax.ShapeDtypeStruct((rows, width), jnp.bfloat16),
         in_specs=specs,
         out_specs=pl.BlockSpec((rows, n), lambda j: (0, j)),
-        scratch_shapes=[pltpu.VMEM((chunks, rows, 256), jnp.bfloat16)],
+        scratch_shapes=[pltpu.VMEM((chunks, rows, 256), jnp.bfloat16)]
+        + [pltpu.VMEM((2 * chunks, n), jnp.float32)] * 4,
         compiler_params=pltpu.CompilerParams(vmem_limit_bytes=48 << 20),
         name="gate_up",
     )(*args)
@@ -125,7 +133,7 @@
     return pl.pallas_call(
         functools.partial(down_kernel, chunks),
         grid=(width // n,),
-        out_shape=jax.ShapeDtypeStruct((rows, width), jnp.float32),
+        out_shape=jax.ShapeDtypeStruct((rows, width), jnp.bfloat16),
         in_specs=[
             pl.BlockSpec((rows, depth), lambda j: (0, 0)),
             words_spec(depth // 16, n),
@@ -133,14 +141,130 @@
             pairs_spec(chunks, n),
         ],
         out_specs=pl.BlockSpec((rows, n), lambda j: (0, j)),
-        scratch_shapes=[pltpu.VMEM((chunks, rows, 256), jnp.bfloat16)],
+        scratch_shapes=[pltpu.VMEM((chunks, rows, 256), jnp.bfloat16)]
+        + [pltpu.VMEM((2 * chunks, n), jnp.float32)] * 2,
         compiler_params=pltpu.CompilerParams(vmem_limit_bytes=48 << 20),
         name="down",
     )(
         x,
         codes.transpose(1, 0, 2),
-        *[v.astype(jnp.float32).reshape(chunks, 2, width) for v in (scale, zero)],
-    )
+        scale,
+        zero,
+    )
+
+
+def greet(partners):
+    barrier = pltpu.get_barrier_semaphore()
+    for partner in partners:
+        pl.semaphore_signal(
+            barrier, inc=1, device_id={"dev": partner}, device_id_type=pl.DeviceIdType.MESH
+        )
+    pl.semaphore_wait(barrier, len(partners))
+
+
+def gather_kernel(outer, x_ref, out_ref, z_send, z_recv, y_send, y_recv, c_send, c_recv, own_sem):
+    me = lax.axis_index("dev")
+    a, y, c = me // 4, (me // 2) % 2, me % 2
+    beside, other = a * 4 + (1 - y) * 2 + c, a * 4 + y * 2 + 1 - c
+
+    def far(d):
+        return lax.rem(a + d, outer)
+
+    def push(src, dst, send, recv, to):
+        copy = pltpu.make_async_remote_copy(
+            src_ref=src,
+            dst_ref=dst,
+            send_sem=send,
+            recv_sem=recv,
+            device_id={"dev": to},
+            device_id_type=pl.DeviceIdType.MESH,
+        )
+        copy.start()
+        return copy
+
+    greet([far(d) * 4 + y * 2 + c for d in range(1, outer)] + [beside, other])
+    own = pltpu.make_async_copy(x_ref, out_ref.at[a, y, c], own_sem)
+    own.start()
+    here = out_ref.at[a, y, c]
+    along = [
+        push(x_ref, here, z_send.at[d], z_recv.at[d], far(d) * 4 + y * 2 + c)
+        for d in range(1, outer)
+    ]
+    sides = [push(x_ref, here, y_send.at[0], y_recv.at[0], beside)]
+    cores = [push(x_ref, here, c_send.at[0], c_recv.at[0], other)]
+    for d in range(1, outer):
+        along[d - 1].wait_recv()
+        block = out_ref.at[far(outer - d), y, c]
+        sides.append(push(block, block, y_send.at[d], y_recv.at[d], beside))
+        cores.append(push(block, block, c_send.at[d], c_recv.at[d], other))
+    for d in range(outer):
+        sides[d].wait_recv()
+        block = out_ref.at[far((outer - d) % outer), 1 - y, c]
+        cores.append(push(block, block, c_send.at[outer + d], c_recv.at[outer + d], other))
+    for copy in cores:
+        copy.wait_recv()
+    for copy in along + sides + cores:
+        copy.wait_send()
+    own.wait()
+
+
+def gather(x, count, number):
+    outer = count // 4
+    dma = pltpu.SemaphoreType.DMA
+    out = pl.pallas_call(
+        functools.partial(gather_kernel, outer),
+        out_shape=jax.ShapeDtypeStruct((outer, 2, 2) + x.shape, x.dtype),
+        in_specs=[pl.BlockSpec(memory_space=pltpu.VMEM)],
+        out_specs=pl.BlockSpec(memory_space=pltpu.VMEM),
+        scratch_shapes=[dma((outer,))] * 4 + [dma((2 * outer,))] * 2 + [dma],
+        compiler_params=pltpu.CompilerParams(
+            collective_id=number, has_side_effects=True, vmem_limit_bytes=48 << 20
+        ),
+        name="gather_%d" % number,
+    )(x)
+    return out.reshape((count,) + x.shape)
+
+
+def scatter_kernel(count, x_ref, own_ref, out_ref, got, send, recv):
+    me = lax.axis_index("dev")
+    to = [lax.rem(me + d, count) for d in range(count)]
+    greet(to[1:])
+    copies = []
+    for d in range(1, count):
+        copy = pltpu.make_async_remote_copy(
+            src_ref=x_ref.at[to[d]],
+            dst_ref=got.at[d],
+            send_sem=send.at[d],
+            recv_sem=recv.at[d],
+            device_id={"dev": to[d]},
+            device_id_type=pl.DeviceIdType.MESH,
+        )
+        copy.start()
+        copies.append(copy)
+    total = own_ref[...].astype(jnp.float32) + x_ref[me].astype(jnp.float32)
+    for d in range(1, count):
+        copies[d - 1].wait_recv()
+        total = total + got[d].astype(jnp.float32)
+    out_ref[...] = total.astype(out_ref.dtype)
+    for copy in copies:
+        copy.wait_send()
+
+
+def scatter_sum(x, own, number):
+    count = x.shape[0]
+    dma = pltpu.SemaphoreType.DMA
+    vmem = pl.BlockSpec(memory_space=pltpu.VMEM)
+    return pl.pallas_call(
+        functools.partial(scatter_kernel, count),
+        out_shape=jax.ShapeDtypeStruct(own.shape, own.dtype),
+        in_specs=[vmem, vmem],
+        out_specs=vmem,
+        scratch_shapes=[pltpu.VMEM(x.shape, x.dtype), dma((count,)), dma((count,))],
+        compiler_params=pltpu.CompilerParams(
+            collective_id=number, has_side_effects=True, vmem_limit_bytes=48 << 20
+        ),
+        name="scatter_%d" % number,
+    )(x, own)
 
 
 def attend_slots(query_rows, incoming_rows, cache_block, lengths):
@@ -218,10 +342,14 @@
     def select_slots(gathered):
         return jnp.dot(chooser, gathered, preferred_element_type=jnp.float32).astype(jnp.bfloat16)
 
-    every_query, every_new, every_stream = (
-        lax.all_gather(query, "dev", axis=0, tiled=True),
-        lax.all_gather(latest_key_value, "dev", axis=0, tiled=True),
-        lax.all_gather(residual, "dev", axis=0, tiled=True),
+    count = lax.axis_size("dev")
+    row_dev, features = residual.shape
+    mine = jnp.concatenate([query, residual, latest_key_value], axis=1)
+    every = gather(mine.reshape(16, -1), count, 0).reshape(count * row_dev, -1)
+    every_query, every_stream, every_new = (
+        every[:, :features],
+        every[:, features : 2 * features],
+        every[:, 2 * features :],
     )
     stream_slots = select_slots(every_stream)
     attended = attend_slots(select_slots(every_query), select_slots(every_new), kv_cache, lengths)
@@ -229,19 +357,21 @@
     slot_stream = (stream_slots.astype(jnp.float32) + attended.astype(jnp.float32)).astype(
         jnp.bfloat16
     )
-    every_slot = lax.all_gather(slot_stream, "dev", axis=0, tiled=True)
-    stream_all = jnp.take(every_slot, owner_map, axis=0)
+    every_slot = gather(slot_stream.reshape(16, -1), count, 1).reshape(-1, features)
+    all_ids = jnp.arange(every_slot.shape[0], dtype=jnp.int32)
+    taker = (owner_map[:, None] == all_ids[None, :]).astype(jnp.bfloat16)
+    stream_all = jnp.dot(taker, every_slot, preferred_element_type=jnp.float32).astype(jnp.bfloat16)
     stream_f = stream_all.astype(jnp.float32)
     mean_square = jnp.mean(stream_f * stream_f, axis=-1, keepdims=True)
     normed = (stream_f * lax.rsqrt(mean_square + 1e-05) * gain_f).astype(jnp.bfloat16)
     activated = gate_up(
-        normed, (gate_codes, gate_scale, gate_zero), (up_codes, up_scale, up_zero), 256
-    )
-    products = down(activated, down_codes, down_scale, down_zero, 512)
-    row_dev = residual.shape[0]
+        normed, (gate_codes, gate_scale, gate_zero), (up_codes, up_scale, up_zero), 512
+    )
+    products = down(activated, down_codes, down_scale, down_zero, 1024)
     own_rows = lax.dynamic_slice_in_dim(stream_all, own_index * row_dev, row_dev, 0)
-    summed = lax.psum_scatter(products, "dev", scatter_dimension=0, tiled=True)
-    return (own_rows.astype(jnp.float32) + summed).astype(jnp.bfloat16)
+    return scatter_sum(
+        products.reshape(count, 16, -1), own_rows.reshape(16, -1), 2
+    ).reshape(row_dev, features)
 
 
 def solution(mesh):

time: 310 us -> 123 us (0.40)
  waiting for transfers between devices: 120 us -> 0 us
  blocking collectives: 63.1 us -> 0 us
  Pallas kernels: 87.6 us -> 111 us
  between operations: 14.3 us -> 0.28 us
  local copies, waits for them, and re-layouts: 16.9 us -> 7.14 us
    unnamed x3 -> x0, waiting for transfers between devices: 91.2 us -> none
    all_gather x3 -> x0, blocking collectives: 63.1 us -> none  [the longest x1 24.9 us: local(): lax.all_gather(query, 'dev', axis=0, tiled=True)]
    pallas_call x0 -> x3, Pallas kernels: none -> 44.8 us  [the longest x2 31.2 us: gather(): pl.pallas_call(functools.partial(gather_kernel, outer), out_shape=jax.Sha...]
    all_gather x1 -> x0, waiting for transfers between devices: 28.5 us -> none  [local(): every_slot = lax.all_gather(slot_stream, 'dev', axis=0, tiled=True)]
    pallas_call x1, Pallas kernels: 58.7 us -> 44.6 us  [gate_up(): pl.pallas_call(functools.partial(gate_up_kernel, chunks), grid=(width //...]
    pallas_call x1, Pallas kernels: 28.8 us -> 21.6 us  [down(): pl.pallas_call(functools.partial(down_kernel, chunks), grid=(width // n,)...]
    reshape x6 -> x5, local copies, waits for them, and re-layouts: 6.78 us -> 0.99 us  [the longest x1 0.63 us: local(): return scatter_sum(products.reshape(count, 16, -1), own_rows.reshape(16,...]
    gather x1 -> x0, local copies, waits for them, and re-layouts: 3.49 us -> none  [local(): stream_all = jnp.take(every_slot, owner_map, axis=0)]
  transfers between devices with their start and end apart: 2 -> 0, of which waited for: 2 -> 0; matrix products, arithmetic and copies ran while one was open for 2% -> 0% of each run, Pallas kernels for 0% -> 0%
where the time goes in v2:
time: 123 us; the launch traced here: 122 us
  Pallas kernels  111 us (90%)
  local copies, waits for them, and re-layouts  7.14 us (6%)
  matrix products  2.06 us (2%)
  other arithmetic  1.38 us (1%)
    pallas_call x1, Pallas kernels, gate_up(): pl.pallas_call(functools.partial(gate_up_kernel, chunks), grid=(width //...  44.6 us
    pallas_call x2, Pallas kernels, gather(): pl.pallas_call(functools.partial(gather_kernel, outer), out_shape=jax.Sha...  31.2 us
    pallas_call x1, Pallas kernels, down(): pl.pallas_call(functools.partial(down_kernel, chunks), grid=(width // n,)...  21.6 us
    pallas_call x1, Pallas kernels, scatter_sum(): pl.pallas_call(functools.partial(scatter_kernel, count), out_shape=jax.Sh...  13.5 us
    unnamed x29, local copies, waits for them, and re-layouts  2.9 us

profile of v2, /device:TPU:0, one launch (start us, length us, event | category | flops | bytes accessed | tf_op | source)
XLA Modules:
  0.0 121.8 jit_solution(9952355076254604558)
XLA Ops:
  0.0 0.9 pad_maximum_fusion
  0.9 16.9 %gather_0.1 = bf16[4,2,2,16,2176]{4,3,2,1,0:T(8,128)(2,1)S(1)} custom-call(bf16[16,2176]{1,0:T(8,128)(2,1)S(1)} %reshape.74.x_ref), custom_call_target="tpu_custom_call" | custom-call | tf_op jit(solution)/shard_map/gather_0/pallas_call | solution.py:214
  17.8 0.6 reshape_reshape.6
  18.4 1.8 %fusion.30 = (bf16[4,256,512]{2,1,0:T(8,128)(2,1)S(1)}, bf16[4,256,512]{2,1,0:T(8,128)(2,1)S(1)}) fusion(bf16[4,256,1024]{2,1,0:T(8,128)(2,1)} %param.19), kind=kLoop, calls=%fused_computation.51 | loop fusion | bytes 4194304 | tf_op jit(solution)/shard_map/slice | solution.py:277
  20.2 1.3 %copy.26 = bf16[4,256,512]{1,2,0:T(8,128)(2,1)} copy(bf16[4,256,512]{2,1,0:T(8,128)(2,1)S(1)} %get-tuple-element.6) | data formatting | bytes 2097152
  21.5 0.2 fusion.5
  21.8 0.2 copy-done.9
  22.1 0.5 copy.25
  22.6 0.3 select_reduce_fusion
  22.9 0.3 copy-done.10
  23.2 0.2 convolution_convert_fusion.3
  23.6 0.2 fusion.11
  23.9 0.4 fusion.4
  24.3 0.3 fusion.2
  24.6 14.4 %gather_1.1 = bf16[4,2,2,16,2048]{4,3,2,1,0:T(8,128)(2,1)S(1)} custom-call(bf16[16,2048]{1,0:T(8,128)(2,1)S(1)} %reshape.79.x_ref), custom_call_target="tpu_custom_call" | custom-call | tf_op jit(solution)/shard_map/gather_1/pallas_call | solution.py:214
  39.0 0.9 reshape_reshape.7
  39.9 0.5 fusion.6
  40.4 0.2 copy-done.7
  40.6 0.2 fusion.8.x_ref
  41.1 44.6 %gate_up.1.x_ref = bf16[32,2048]{1,0:T(8,128)(2,1)S(1)} custom-call(bf16[32,8192]{1,0:T(8,128)(2,1)S(1)} %fusion.8.x_ref, f32[3,512,2048]{2,1,0:T(8,128)} %bitcast.25, bf16[64,2048]{1,0:T(8,128)(2,1)S(1)} %copy-done, bf16[64,2048]{1,0:T(8,128)(2,1)S(1)} %copy-done.1, f32[3,512,2048]{2,1,0:T(8,128)} %bitcast.26, bf16[64,2048]{1,0:T(8,128)(2,1)S(1)} %copy-done.2, ...), custom_call_target="tpu_custom_call" | custom-call | tf_op jit(solution)/shard_map/gate_up/pallas_call | solution.py:116
  85.8 21.6 %down.1 = bf16[32,8192]{1,0:T(8,128)(2,1)S(1)} custom-call(bf16[32,2048]{1,0:T(8,128)(2,1)S(1)} %gate_up.1.x_ref, f32[3,128,8192]{2,1,0:T(8,128)} %bitcast.27, bf16[16,8192]{1,0:T(8,128)(2,1)S(1)} %copy-done.4, bf16[16,8192]{1,0:T(8,128)(2,1)S(1)} %copy-done.5), custom_call_target="tpu_custom_call" | custom-call | tf_op jit(solution)/shard_map/down/pallas_call | solution.py:133
  107.3 0.2 reshape.80.x_ref
  107.6 13.5 %scatter_2.1 = bf16[16,1024]{1,0:T(8,128)(2,1)S(1)} custom-call(bf16[16,16,1024]{2,1,0:T(8,128)(2,1)S(1)} %reshape.80.x_ref, bf16[16,1024]{1,0:T(8,128)(2,1)S(1)} %reshape.81.own_ref), custom_call_target="tpu_custom_call" | custom-call | tf_op jit(solution)/shard_map/scatter_2/pallas_call | solution.py:257
  121.2 0.6 reshape.82
  (38 shorter events, 0.8 us)
Async XLA Ops:
  20.1 1.3 %copy-start.12 = (s32[4]{0:T(128)S(1)}, s32[4]{0:T(128)}, u32[]{:S(2)}) copy-start(s32[4]{0:T(128)} %param.20) | copy-start | bytes 52
  20.2 1.4 %copy-start.8 = (s32[32]{0:T(128)S(1)}, s32[32]{0:T(128)}, u32[]{:S(2)}) copy-start(s32[32]{0:T(128)} %param.21) | copy-start | bytes 388
  21.5 0.5 copy-start.9
  22.6 0.7 copy-start.10
  22.6 1.3 %copy-start.6 = (bf16[4,256,512]{1,2,0:T(8,128)(2,1)S(1)}, bf16[4,256,512]{1,2,0:T(8,128)(2,1)}, u32[]{:S(2)}) copy-start(bf16[4,256,512]{1,2,0:T(8,128)(2,1)} %copy.26) | copy-start | bytes 3145732
  23.6 0.7 copy-start.11
  39.9 0.7 copy-start.7
  39.9 1.0 copy-start
  39.9 1.0 copy-start.1
  39.9 1.1 copy-start.2
  39.9 1.2 copy-start.3
  41.1 44.6 %copy-start.4 = (bf16[16,8192]{1,0:T(8,128)(2,1)S(1)}, bf16[16,8192]{1,0:T(8,128)(2,1)}, u32[]{:S(2)}) copy-start(bf16[16,8192]{1,0:T(8,128)(2,1)} %s_in.1) | copy-start | bytes 786436
  41.1 44.6 %copy-start.5 = (bf16[16,8192]{1,0:T(8,128)(2,1)S(1)}, bf16[16,8192]{1,0:T(8,128)(2,1)}, u32[]{:S(2)}) copy-start(bf16[16,8192]{1,0:T(8,128)(2,1)} %z_in.1) | copy-start | bytes 786436

commit v3 on v2

--- a/solution.py
+++ b/solution.py
@@ -74,24 +74,61 @@
         return tuple(new)
 
     start = jnp.zeros((rows, n), jnp.float32)
-    gate, up = lax.fori_loop(0, chunks, step, (start, start))
+    gate, up = lax.fori_loop(0, chunks, step, (start, start), unroll=min(8, chunks))
     out_ref[...] = (gate / (1.0 + jnp.exp(-gate)) * up).astype(jnp.bfloat16)
 
 
-def down_kernel(chunks, x_ref, c, s_in, z_in, out_ref, xp_ref, s, z):
-    rows, n = out_ref.shape
+def down_kernel(
+    chunks, count, x_ref, c, s_in, z_in, own_ref, out_ref, xp_ref, s, z, mine, got, send, recv
+):
+    rows, n = x_ref.shape[0], s.shape[1]
+    each = rows // count
+    j, steps = pl.program_id(0), pl.num_programs(0)
+    me = lax.axis_index("dev")
+    to = [lax.rem(me + d, count) for d in range(count)]
     widen((s_in, z_in), (s, z))
 
-    @pl.when(pl.program_id(0) == 0)
+    def copy(tile, d):
+        return pltpu.make_async_remote_copy(
+            src_ref=mine.at[tile, to[d]],
+            dst_ref=got.at[tile, d],
+            send_sem=send.at[tile, d],
+            recv_sem=recv.at[tile, d],
+            device_id={"dev": to[d]},
+            device_id_type=pl.DeviceIdType.MESH,
+        )
+
+    @pl.when(j == 0)
     def _():
+        greet(to[1:])
         reorder(x_ref, xp_ref, chunks)
 
     def step(t, total):
         w = unpack_chunk(c, t, rows_of(s, t, n), rows_of(z, t, n))
         return total + jnp.dot(xp_ref[t], w, preferred_element_type=jnp.float32)
 
-    total = lax.fori_loop(0, chunks, step, jnp.zeros((rows, n), jnp.float32))
-    out_ref[...] = total.astype(jnp.bfloat16)
+    start = jnp.zeros((rows, n), jnp.float32)
+    total = lax.fori_loop(0, chunks, step, start, unroll=min(8, chunks))
+    total = total.astype(jnp.bfloat16)
+    for d in range(count):
+        mine[j, d] = total[each * d : each * (d + 1), :]
+    for d in range(1, count):
+        copy(j, d).start()
+
+    @pl.when(j == steps - 1)
+    def _():
+        def finish(tile, carry):
+            here = pl.ds(pl.multiple_of(tile * n, n), n)
+            summed = own_ref[:, here].astype(jnp.float32) + mine[tile, me].astype(jnp.float32)
+            for d in range(1, count):
+                copy(tile, d).wait_recv()
+                summed = summed + got[tile, d].astype(jnp.float32)
+            out_ref[:, here] = summed.astype(jnp.bfloat16)
+            for d in range(1, count):
+                copy(tile, d).wait_send()
+            return carry
+
+        lax.fori_loop(0, steps, finish, 0)
 
 
 def words_spec(words, n):
@@ -126,31 +163,33 @@
     )(*args)
 
 
-def down(x, codes, scale, zero, n):
+def down(x, codes, scale, zero, own, count, n, number):
     rows, depth = x.shape
     width = codes.shape[2]
     chunks = depth // 256
+    steps = width // n
+    dma = pltpu.SemaphoreType.DMA
+    blocks = pltpu.VMEM((steps, count, rows // count, n), jnp.bfloat16)
     return pl.pallas_call(
-        functools.partial(down_kernel, chunks),
-        grid=(width // n,),
-        out_shape=jax.ShapeDtypeStruct((rows, width), jnp.bfloat16),
+        functools.partial(down_kernel, chunks, count),
+        grid=(steps,),
+        out_shape=jax.ShapeDtypeStruct(own.shape, own.dtype),
         in_specs=[
             pl.BlockSpec((rows, depth), lambda j: (0, 0)),
             words_spec(depth // 16, n),
             pairs_spec(chunks, n),
             pairs_spec(chunks, n),
+            pl.BlockSpec(own.shape, lambda j: (0, 0)),
         ],
-        out_specs=pl.BlockSpec((rows, n), lambda j: (0, j)),
+        out_specs=pl.BlockSpec(own.shape, lambda j: (0, 0)),
         scratch_shapes=[pltpu.VMEM((chunks, rows, 256), jnp.bfloat16)]
-        + [pltpu.VMEM((2 * chunks, n), jnp.float32)] * 2,
-        compiler_params=pltpu.CompilerParams(vmem_limit_bytes=48 << 20),
+        + [pltpu.VMEM((2 * chunks, n), jnp.float32)] * 2
+        + [blocks, blocks, dma((steps, count)), dma((steps, count))],
+        compiler_params=pltpu.CompilerParams(
+            collective_id=number, has_side_effects=True, vmem_limit_bytes=48 << 20
+        ),
         name="down",
-    )(
-        x,
-        codes.transpose(1, 0, 2),
-        scale,
-        zero,
-    )
+    )(x, codes.transpose(1, 0, 2), scale, zero, own)
 
 
 def greet(partners):
@@ -225,48 +264,6 @@
     return out.reshape((count,) + x.shape)
 
 
-def scatter_kernel(count, x_ref, own_ref, out_ref, got, send, recv):
-    me = lax.axis_index("dev")
-    to = [lax.rem(me + d, count) for d in range(count)]
-    greet(to[1:])
-    copies = []
-    for d in range(1, count):
-        copy = pltpu.make_async_remote_copy(
-            src_ref=x_ref.at[to[d]],
-            dst_ref=got.at[d],
-            send_sem=send.at[d],
-            recv_sem=recv.at[d],
-            device_id={"dev": to[d]},
-            device_id_type=pl.DeviceIdType.MESH,
-        )
-        copy.start()
-        copies.append(copy)
-    total = own_ref[...].astype(jnp.float32) + x_ref[me].astype(jnp.float32)
-    for d in range(1, count):
-        copies[d - 1].wait_recv()
-        total = total + got[d].astype(jnp.float32)
-    out_ref[...] = total.astype(out_ref.dtype)
-    for copy in copies:
-        copy.wait_send()
-
-
-def scatter_sum(x, own, number):
-    count = x.shape[0]
-    dma = pltpu.SemaphoreType.DMA
-    vmem = pl.BlockSpec(memory_space=pltpu.VMEM)
-    return pl.pallas_call(
-        functools.partial(scatter_kernel, count),
-        out_shape=jax.ShapeDtypeStruct(own.shape, own.dtype),
-        in_specs=[vmem, vmem],
-        out_specs=vmem,
-        scratch_shapes=[pltpu.VMEM(x.shape, x.dtype), dma((count,)), dma((count,))],
-        compiler_params=pltpu.CompilerParams(
-            collective_id=number, has_side_effects=True, vmem_limit_bytes=48 << 20
-        ),
-        name="scatter_%d" % number,
-    )(x, own)
-
-
 def attend_slots(query_rows, incoming_rows, cache_block, lengths):
     count_of_slots = query_rows.shape[0]
     context_span = cache_block.shape[1]
@@ -367,11 +364,8 @@
     activated = gate_up(
         normed, (gate_codes, gate_scale, gate_zero), (up_codes, up_scale, up_zero), 512
     )
-    products = down(activated, down_codes, down_scale, down_zero, 1024)
     own_rows = lax.dynamic_slice_in_dim(stream_all, own_index * row_dev, row_dev, 0)
-    return scatter_sum(
-        products.reshape(count, 16, -1), own_rows.reshape(16, -1), 2
-    ).reshape(row_dev, features)
+    return down(activated, down_codes, down_scale, down_zero, own_rows, count, 1024, 2)
 
 
 def solution(mesh):

time: 123 us -> 97.6 us (0.79)
  Pallas kernels: 111 us -> 86.7 us
    pallas_call x1, Pallas kernels: 44.6 us -> 30.9 us  [gate_up(): pl.pallas_call(functools.partial(gate_up_kernel, chunks), grid=(width //...]
    pallas_call x2 -> x1, Pallas kernels: 35.1 us -> 24.6 us  [down(): pl.pallas_call(functools.partial(down_kernel, chunks, count), grid=(steps...]
    unnamed x29 -> x30, local copies, waits for them, and re-layouts: 2.9 us -> 3.52 us
where the time goes in v3:
time: 97.6 us; the launch traced here: 97.3 us
  Pallas kernels  86.7 us (89%)
  local copies, waits for them, and re-layouts  6.86 us (7%)
  matrix products  2.06 us (2%)
  other arithmetic  1.38 us (1%)
    pallas_call x2, Pallas kernels, gather(): pl.pallas_call(functools.partial(gather_kernel, outer), out_shape=jax.Sha...  31.2 us
    pallas_call x1, Pallas kernels, gate_up(): pl.pallas_call(functools.partial(gate_up_kernel, chunks), grid=(width //...  30.9 us
    pallas_call x1, Pallas kernels, down(): pl.pallas_call(functools.partial(down_kernel, chunks, count), grid=(steps...  24.6 us
    unnamed x30, local copies, waits for them, and re-layouts  3.52 us

profile of v3, /device:TPU:0, one launch (start us, length us, event | category | flops | bytes accessed | tf_op | source)
XLA Modules:
  0.0 97.3 jit_solution(392044366334922935)
XLA Ops:
  0.0 0.9 pad_maximum_fusion
  0.9 16.9 %gather_0.1 = bf16[4,2,2,16,2176]{4,3,2,1,0:T(8,128)(2,1)S(1)} custom-call(bf16[16,2176]{1,0:T(8,128)(2,1)S(1)} %reshape.65.x_ref), custom_call_target="tpu_custom_call" | custom-call | tf_op jit(solution)/shard_map/gather_0/pallas_call | solution.py:253
  17.8 0.6 reshape_reshape.6
  18.4 1.8 %fusion.30 = (bf16[4,256,512]{2,1,0:T(8,128)(2,1)S(1)}, bf16[4,256,512]{2,1,0:T(8,128)(2,1)S(1)}) fusion(bf16[4,256,1024]{2,1,0:T(8,128)(2,1)} %param.19), kind=kLoop, calls=%fused_computation.51 | loop fusion | bytes 4194304 | tf_op jit(solution)/shard_map/slice | solution.py:274
  20.2 1.3 %copy.26 = bf16[4,256,512]{1,2,0:T(8,128)(2,1)} copy(bf16[4,256,512]{2,1,0:T(8,128)(2,1)S(1)} %get-tuple-element.6) | data formatting | bytes 2097152
  21.5 0.2 fusion.5
  21.8 0.2 copy-done.9
  22.1 0.5 copy.25
  22.6 0.3 select_reduce_fusion
  22.9 0.3 copy-done.10
  23.2 0.2 convolution_convert_fusion.3
  23.4 0.1 fusion.31
  23.6 0.2 fusion.11
  23.9 0.4 fusion.4
  24.3 0.3 fusion.2
  24.6 14.4 %gather_1.1 = bf16[4,2,2,16,2048]{4,3,2,1,0:T(8,128)(2,1)S(1)} custom-call(bf16[16,2048]{1,0:T(8,128)(2,1)S(1)} %reshape.70.x_ref), custom_call_target="tpu_custom_call" | custom-call | tf_op jit(solution)/shard_map/gather_1/pallas_call | solution.py:253
  39.0 0.9 reshape_reshape.7
  39.9 0.5 fusion.6
  40.4 0.2 copy-done.7
  40.6 0.2 fusion.8.x_ref
  40.9 0.1 copy-done.2
  41.1 30.9 %gate_up.1.x_ref = bf16[32,2048]{1,0:T(8,128)(2,1)S(1)} custom-call(bf16[32,8192]{1,0:T(8,128)(2,1)S(1)} %fusion.8.x_ref, f32[3,512,2048]{2,1,0:T(8,128)} %bitcast.25, bf16[64,2048]{1,0:T(8,128)(2,1)S(1)} %copy-done, bf16[64,2048]{1,0:T(8,128)(2,1)S(1)} %copy-done.1, f32[3,512,2048]{2,1,0:T(8,128)} %bitcast.26, bf16[64,2048]{1,0:T(8,128)(2,1)S(1)} %copy-done.2, ...), custom_call_target="tpu_custom_call" | custom-call | tf_op jit(solution)/shard_map/gate_up/pallas_call | solution.py:153
  72.1 24.6 %down.1 = bf16[2,8192]{1,0:T(2,128)(2,1)S(1)} custom-call(bf16[32,2048]{1,0:T(8,128)(2,1)S(1)} %gate_up.1.x_ref, f32[3,128,8192]{2,1,0:T(8,128)} %bitcast.27, bf16[16,8192]{1,0:T(8,128)(2,1)S(1)} %copy-done.4, bf16[16,8192]{1,0:T(8,128)(2,1)S(1)} %copy-done.5, bf16[2,8192]{1,0:T(2,128)(2,1)S(1)} %constant_dynamic-slice_fusion.own_ref), custom_call_target="tpu_custom_call" | custom-call | tf_op jit(solution)/shard_map/down/pallas_call | solution.py:173
  96.7 0.6 copy.31
  (35 shorter events, 0.6 us)
Async XLA Ops:
  20.1 1.3 %copy-start.12 = (s32[4]{0:T(128)S(1)}, s32[4]{0:T(128)}, u32[]{:S(2)}) copy-start(s32[4]{0:T(128)} %param.20) | copy-start | bytes 52
  20.2 1.4 %copy-start.8 = (s32[32]{0:T(128)S(1)}, s32[32]{0:T(128)}, u32[]{:S(2)}) copy-start(s32[32]{0:T(128)} %param.21) | copy-start | bytes 388
  21.5 0.5 copy-start.9
  22.6 0.7 copy-start.10
  22.6 1.3 %copy-start.6 = (bf16[4,256,512]{1,2,0:T(8,128)(2,1)S(1)}, bf16[4,256,512]{1,2,0:T(8,128)(2,1)}, u32[]{:S(2)}) copy-start(bf16[4,256,512]{1,2,0:T(8,128)(2,1)} %copy.26) | copy-start | bytes 3145732
  23.6 0.7 copy-start.11
  39.9 0.7 copy-start.7
  39.9 1.0 copy-start
  39.9 1.0 %copy-start.1 = (bf16[64,2048]{1,0:T(8,128)(2,1)S(1)}, bf16[64,2048]{1,0:T(8,128)(2,1)}, u32[]{:S(2)}) copy-start(bf16[64,2048]{1,0:T(8,128)(2,1)} %gz_in.1) | copy-start | bytes 786436
  39.9 1.1 %copy-start.2 = (bf16[64,2048]{1,0:T(8,128)(2,1)S(1)}, bf16[64,2048]{1,0:T(8,128)(2,1)}, u32[]{:S(2)}) copy-start(bf16[64,2048]{1,0:T(8,128)(2,1)} %us_in.1) | copy-start | bytes 786436
  39.9 1.2 %copy-start.3 = (bf16[64,2048]{1,0:T(8,128)(2,1)S(1)}, bf16[64,2048]{1,0:T(8,128)(2,1)}, u32[]{:S(2)}) copy-start(bf16[64,2048]{1,0:T(8,128)(2,1)} %uz_in.1) | copy-start | bytes 786436
  41.1 31.0 %copy-start.4 = (bf16[16,8192]{1,0:T(8,128)(2,1)S(1)}, bf16[16,8192]{1,0:T(8,128)(2,1)}, u32[]{:S(2)}) copy-start(bf16[16,8192]{1,0:T(8,128)(2,1)} %s_in.1) | copy-start | bytes 786436
  41.1 31.0 %copy-start.5 = (bf16[16,8192]{1,0:T(8,128)(2,1)S(1)}, bf16[16,8192]{1,0:T(8,128)(2,1)}, u32[]{:S(2)}) copy-start(bf16[16,8192]{1,0:T(8,128)(2,1)} %z_in.1) | copy-start | bytes 786436

commit v4 on v3

--- a/solution.py
+++ b/solution.py
@@ -365,7 +365,7 @@
         normed, (gate_codes, gate_scale, gate_zero), (up_codes, up_scale, up_zero), 512
     )
     own_rows = lax.dynamic_slice_in_dim(stream_all, own_index * row_dev, row_dev, 0)
-    return down(activated, down_codes, down_scale, down_zero, own_rows, count, 1024, 2)
+    return down(activated, down_codes, down_scale, down_zero, own_rows, count, 2048, 2)
 
 
 def solution(mesh):

time: 97.6 us -> 96.5 us (0.989)
  Pallas kernels: 86.7 us -> 85.7 us
    pallas_call x1, Pallas kernels: 24.6 us -> 23.5 us  [down(): pl.pallas_call(functools.partial(down_kernel, chunks, count), grid=(steps...]
where the time goes in v4:
time: 96.5 us; the launch traced here: 96.3 us
  Pallas kernels  85.7 us (89%)
  local copies, waits for them, and re-layouts  6.86 us (7%)
  matrix products  2.06 us (2%)
  other arithmetic  1.38 us (1%)
    pallas_call x2, Pallas kernels, gather(): pl.pallas_call(functools.partial(gather_kernel, outer), out_shape=jax.Sha...  31.2 us
    pallas_call x1, Pallas kernels, gate_up(): pl.pallas_call(functools.partial(gate_up_kernel, chunks), grid=(width //...  30.9 us
    pallas_call x1, Pallas kernels, down(): pl.pallas_call(functools.partial(down_kernel, chunks, count), grid=(steps...  23.5 us
    unnamed x30, local copies, waits for them, and re-layouts  3.52 us

profile of v4, /device:TPU:0, one launch (start us, length us, event | category | flops | bytes accessed | tf_op | source)
XLA Modules:
  0.0 96.3 jit_solution(4056041825430636976)
XLA Ops:
  0.0 0.9 pad_maximum_fusion
  0.9 16.9 %gather_0.1 = bf16[4,2,2,16,2176]{4,3,2,1,0:T(8,128)(2,1)S(1)} custom-call(bf16[16,2176]{1,0:T(8,128)(2,1)S(1)} %reshape.65.x_ref), custom_call_target="tpu_custom_call" | custom-call | tf_op jit(solution)/shard_map/gather_0/pallas_call | solution.py:253
  17.8 0.6 reshape_reshape.6
  18.4 1.8 %fusion.30 = (bf16[4,256,512]{2,1,0:T(8,128)(2,1)S(1)}, bf16[4,256,512]{2,1,0:T(8,128)(2,1)S(1)}) fusion(bf16[4,256,1024]{2,1,0:T(8,128)(2,1)} %param.19), kind=kLoop, calls=%fused_computation.51 | loop fusion | bytes 4194304 | tf_op jit(solution)/shard_map/slice | solution.py:274
  20.2 1.3 %copy.26 = bf16[4,256,512]{1,2,0:T(8,128)(2,1)} copy(bf16[4,256,512]{2,1,0:T(8,128)(2,1)S(1)} %get-tuple-element.6) | data formatting | bytes 2097152
  21.5 0.2 fusion.5
  21.8 0.2 copy-done.9
  22.1 0.5 copy.25
  22.6 0.3 select_reduce_fusion
  22.9 0.3 copy-done.10
  23.2 0.2 convolution_convert_fusion.3
  23.4 0.1 fusion.31
  23.6 0.2 fusion.11
  23.9 0.4 fusion.4
  24.3 0.3 fusion.2
  24.6 14.4 %gather_1.1 = bf16[4,2,2,16,2048]{4,3,2,1,0:T(8,128)(2,1)S(1)} custom-call(bf16[16,2048]{1,0:T(8,128)(2,1)S(1)} %reshape.70.x_ref), custom_call_target="tpu_custom_call" | custom-call | tf_op jit(solution)/shard_map/gather_1/pallas_call | solution.py:253
  39.0 0.9 reshape_reshape.7
  39.9 0.5 fusion.6
  40.4 0.2 copy-done.7
  40.6 0.2 fusion.8.x_ref
  40.9 0.1 copy-done.2
  41.1 30.9 %gate_up.1.x_ref = bf16[32,2048]{1,0:T(8,128)(2,1)S(1)} custom-call(bf16[32,8192]{1,0:T(8,128)(2,1)S(1)} %fusion.8.x_ref, f32[3,512,2048]{2,1,0:T(8,128)} %bitcast.25, bf16[64,2048]{1,0:T(8,128)(2,1)S(1)} %copy-done, bf16[64,2048]{1,0:T(8,128)(2,1)S(1)} %copy-done.1, f32[3,512,2048]{2,1,0:T(8,128)} %bitcast.26, bf16[64,2048]{1,0:T(8,128)(2,1)S(1)} %copy-done.2, ...), custom_call_target="tpu_custom_call" | custom-call | tf_op jit(solution)/shard_map/gate_up/pallas_call | solution.py:153
  72.1 23.5 %down.1 = bf16[2,8192]{1,0:T(2,128)(2,1)S(1)} custom-call(bf16[32,2048]{1,0:T(8,128)(2,1)S(1)} %gate_up.1.x_ref, f32[3,128,8192]{2,1,0:T(8,128)} %bitcast.27, bf16[16,8192]{1,0:T(8,128)(2,1)S(1)} %copy-done.4, bf16[16,8192]{1,0:T(8,128)(2,1)S(1)} %copy-done.5, bf16[2,8192]{1,0:T(2,128)(2,1)S(1)} %constant_dynamic-slice_fusion.own_ref), custom_call_target="tpu_custom_call" | custom-call | tf_op jit(solution)/shard_map/down/pallas_call | solution.py:173
  95.6 0.6 copy.31
  (35 shorter events, 0.6 us)
Async XLA Ops:
  20.1 1.3 %copy-start.12 = (s32[4]{0:T(128)S(1)}, s32[4]{0:T(128)}, u32[]{:S(2)}) copy-start(s32[4]{0:T(128)} %param.20) | copy-start | bytes 52
  20.2 1.4 %copy-start.8 = (s32[32]{0:T(128)S(1)}, s32[32]{0:T(128)}, u32[]{:S(2)}) copy-start(s32[32]{0:T(128)} %param.21) | copy-start | bytes 388
  21.5 0.5 copy-start.9
  22.6 0.7 copy-start.10
  22.6 1.3 %copy-start.6 = (bf16[4,256,512]{1,2,0:T(8,128)(2,1)S(1)}, bf16[4,256,512]{1,2,0:T(8,128)(2,1)}, u32[]{:S(2)}) copy-start(bf16[4,256,512]{1,2,0:T(8,128)(2,1)} %copy.26) | copy-start | bytes 3145732
  23.6 0.7 copy-start.11
  39.9 0.7 copy-start.7
  39.9 1.0 copy-start
  39.9 1.0 %copy-start.1 = (bf16[64,2048]{1,0:T(8,128)(2,1)S(1)}, bf16[64,2048]{1,0:T(8,128)(2,1)}, u32[]{:S(2)}) copy-start(bf16[64,2048]{1,0:T(8,128)(2,1)} %gz_in.1) | copy-start | bytes 786436
  39.9 1.1 %copy-start.2 = (bf16[64,2048]{1,0:T(8,128)(2,1)S(1)}, bf16[64,2048]{1,0:T(8,128)(2,1)}, u32[]{:S(2)}) copy-start(bf16[64,2048]{1,0:T(8,128)(2,1)} %us_in.1) | copy-start | bytes 786436
  39.9 1.2 %copy-start.3 = (bf16[64,2048]{1,0:T(8,128)(2,1)S(1)}, bf16[64,2048]{1,0:T(8,128)(2,1)}, u32[]{:S(2)}) copy-start(bf16[64,2048]{1,0:T(8,128)(2,1)} %uz_in.1) | copy-start | bytes 786436
  41.1 31.0 %copy-start.4 = (bf16[16,8192]{1,0:T(8,128)(2,1)S(1)}, bf16[16,8192]{1,0:T(8,128)(2,1)}, u32[]{:S(2)}) copy-start(bf16[16,8192]{1,0:T(8,128)(2,1)} %s_in.1) | copy-start | bytes 786436
  41.1 31.0 %copy-start.5 = (bf16[16,8192]{1,0:T(8,128)(2,1)S(1)}, bf16[16,8192]{1,0:T(8,128)(2,1)}, u32[]{:S(2)}) copy-start(bf16[16,8192]{1,0:T(8,128)(2,1)} %z_in.1) | copy-start | bytes 786436
